TPU v7x, 32 devices: a whole 2x2x4 slice. The times are simulated.
32 devices in a mesh: adv: 16 (over z, y, core), imp: 2 (over x).
Axes of the slice: x: 2, y: 2, z: 4, core: 2. Of those that a mesh axis runs over, the one named last changes fastest.
Arguments:
- values: bfloat16 [4096, 16384], P('adv', 'imp'), may hold values from 0 to 4
- limits: float32 [4096], P('adv'), may hold values from 0.05 to 3
- start_pace: float32 [4096], P('adv'), may hold values from 0.3 to 1
- reserve: float32 [16384], P('imp'), may hold values from 0.2 to 1.2
Outputs:
- pace: float32 [4096], P('adv')
- prices: float32 [16384], P('imp')
All inputs are finite; a program needn't handle non-finite values.
Results may differ from a plain program's by a relative error of at most 0.0003.
Values sent between devices are 32-bit elements; how exact they have to be, the bound alone decides.
A program may use at most 64 MiB of HBM per device.

v0:
```python
import jax
import jax.numpy as jnp
from jax import lax
from jax.sharding import PartitionSpec as P

ROUNDS = 2


EPS = 0.015


def merged(value, axis, join):
    pieces = jax.tree.map(lambda part: lax.all_gather(part, axis), value)
    head = jax.tree.map(lambda part: part[0], pieces)
    tail = jax.tree.map(lambda part: part[1:], pieces)
    subtotal, _ = lax.scan(lambda subtotal, slab: (join(subtotal, slab), None), head, tail)
    return subtotal


def combine_pair(first, second):
    top = jnp.maximum(first[0], second[0])
    return (top, first[1] * jnp.exp(first[0] - top) + second[1] * jnp.exp(second[0] - top))


def log_totals(score, rlog):
    local_top = jnp.max(score, axis=0)
    local_sum = jnp.sum(jnp.exp(score - local_top[None, :]), axis=0)
    top, total = merged((local_top, local_sum), "adv", combine_pair)
    upper = jnp.maximum(top, rlog)
    whole = total * jnp.exp(top - upper) + jnp.exp(rlog - upper)
    return upper + jnp.log(whole)


def update_pace(partial_value, pace, limits):
    spend = lax.psum(partial_value, "imp")
    return jnp.minimum(1.0, pace * jnp.sqrt(limits / spend))


def on_device(values, limits, start_pace, reserve):
    pace = start_pace
    rlog = reserve / EPS
    prices = jnp.zeros_like(reserve)
    for step in range(ROUNDS):
        bid = pace[:, None] * values.astype(jnp.float32)
        score = bid / EPS
        lse = log_totals(score, rlog)
        prices = EPS * lse
        partial_value = jnp.sum(jnp.exp(score - lse[None, :]) * bid, axis=1)
        pace = update_pace(partial_value, pace, limits)
    return (pace, prices)


def solution(mesh):
    placed = (P("adv", "imp"), P("adv"), P("adv"), P("imp"))
    return jax.shard_map(
        on_device, mesh=mesh, in_specs=placed, out_specs=(P("adv"), P("imp")), check_vma=False
    )
```

profile of v0, /device:TPU:0, one launch (start us, length us, event | category | flops | bytes accessed | tf_op | source)
XLA Modules:
  0.0 117.9 jit_solution(5938012003814389603)
XLA Ops:
  0.7 3.6 %fusion.4 = f32[8192]{0:T(1024)S(1)} fusion(bf16[256,8192]{1,0:T(8,128)(2,1)} %param.8, f32[256]{0:T(256)} %param.10), kind=kLoop, calls=%fused_computation.12 | loop fusion | flops 8380416 | bytes 4228096 | tf_op jit(solution)/shard_map/reduce_max | solution.py:26
  4.2 2.0 %fusion.15 = f32[8192]{0:T(1024)S(1)} fusion(bf16[256,8192]{1,0:T(8,128)(2,1)S(1)} %copy-done, f32[8192]{0:T(1024)S(1)} %fusion.4, f32[256]{0:T(256)S(1)} %copy-done.3), kind=kLoop, calls=%fused_computation.23 | loop fusion | flops 10477568 | bytes 4260864 | tf_op jit(solution)/shard_map/reduce_sum | solution.py:27
  6.3 24.6 %all-gather = f32[131072]{0:T(1024)S(1)} all-gather(f32[8192]{0:T(1024)S(1)} %fusion.4), channel_id=2, replica_groups=mesh['adv'=16,'imp'=2] {'adv'}, dimensions={0}, use_global_device_ids=true | all-gather | bytes 557056 | tf_op jit(solution)/shard_map/all_gather | solution.py:13
  30.9 0.1 reshape.18
  31.0 18.9 %all-gather.1 = f32[131072]{0:T(1024)S(1)} all-gather(f32[8192]{0:T(1024)S(1)} %fusion.15), channel_id=3, replica_groups=mesh['adv'=16,'imp'=2] {'adv'}, dimensions={0}, use_global_device_ids=true | all-gather | bytes 557056 | tf_op jit(solution)/shard_map/all_gather | solution.py:13
  49.9 0.1 reshape.19
  50.0 1.7 %while.24 = (s32[]{:T(128)}, f32[8192]{0:T(1024)S(1)}, f32[8192]{0:T(1024)S(1)}, f32[15,8192]{1,0:T(8,128)S(1)}, f32[15,8192]{1,0:T(8,128)S(1)}, /*index=5*/s32[]{:T(128)}) while((s32[]{:T(128)}, f32[8192]{0:T(1024)S(1)}, f32[8192]{0:T(1024)S(1)}, f32[15,8192]{1,0:T(8,128)S(1)}, f32[15,8192]{1,0:T(8,128)S(1)}, /*index=5*/s32[]{:T(128)}) %tuple.48), condition=%wide.region_3.4_spmd, body=%wide.region_2.3_spmd.sunk | while | flops 49154 | bytes 327761 | solution.py:16
  50.0 0.1 constant_dynamic-slice_fusion.6
  50.1 0.1 constant_dynamic-slice_fusion.6
  50.3 0.1 constant_dynamic-slice_fusion.6
  50.4 0.1 constant_dynamic-slice_fusion.6
  50.5 0.1 constant_dynamic-slice_fusion.6
  50.6 0.1 constant_dynamic-slice_fusion.6
  50.7 0.1 constant_dynamic-slice_fusion.6
  50.8 0.1 constant_dynamic-slice_fusion.6
  51.0 0.1 constant_dynamic-slice_fusion.6
  51.1 0.1 constant_dynamic-slice_fusion.6
  51.2 0.1 constant_dynamic-slice_fusion.6
  51.3 0.1 constant_dynamic-slice_fusion.6
  51.8 4.1 %fusion.17 = f32[256]{0:T(256)S(1)} fusion(bf16[256,8192]{1,0:T(8,128)(2,1)} %param.8, f32[8192]{0:T(1024)S(1)} %log_add_fusion.1, f32[256]{0:T(256)S(1)} %copy-done.3), kind=kLoop, calls=%fused_computation.25 | loop fusion | flops 12582656 | bytes 4229120 | tf_op jit(solution)/shard_map/reduce_sum | solution.py:48
  55.9 4.9 %psum.14 = f32[256]{0:T(256)S(1)} all-reduce(f32[256]{0:T(256)S(1)} %fusion.17), channel_id=1, replica_groups=mesh['adv'=16,'imp'=2] {'imp'}, use_global_device_ids=true, to_apply=%region_5.6 | all-reduce | flops 256 | bytes 2048 | tf_op jit(solution)/shard_map/psum | solution.py:35
  60.9 3.6 %fusion.9 = f32[8192]{0:T(1024)S(1)} fusion(bf16[256,8192]{1,0:T(8,128)(2,1)} %param.8, f32[256]{0:T(256)S(1)} %multiply_minimum_fusion.1), kind=kLoop, calls=%fused_computation.17 | loop fusion | flops 8380416 | bytes 4228096 | tf_op jit(solution)/shard_map/reduce_max | solution.py:26
  64.5 2.0 %fusion.11 = f32[8192]{0:T(1024)S(1)} fusion(bf16[256,8192]{1,0:T(8,128)(2,1)S(1)} %copy-done.1, f32[8192]{0:T(1024)S(1)} %fusion.9, f32[256]{0:T(256)S(1)} %multiply_minimum_fusion.1), kind=kLoop, calls=%fused_computation.19 | loop fusion | flops 10477568 | bytes 4260864 | tf_op jit(solution)/shard_map/reduce_sum | solution.py:27
  66.5 20.2 %all-gather.2 = f32[131072]{0:T(1024)S(1)} all-gather(f32[8192]{0:T(1024)S(1)} %fusion.9), channel_id=4, replica_groups=mesh['adv'=16,'imp'=2] {'adv'}, dimensions={0}, use_global_device_ids=true | all-gather | bytes 557056 | tf_op jit(solution)/shard_map/all_gather | solution.py:13
  86.8 0.1 reshape.24
  86.9 18.9 %all-gather.3 = f32[131072]{0:T(1024)S(1)} all-gather(f32[8192]{0:T(1024)S(1)} %fusion.11), channel_id=5, replica_groups=mesh['adv'=16,'imp'=2] {'adv'}, dimensions={0}, use_global_device_ids=true | all-gather | bytes 557056 | tf_op jit(solution)/shard_map/all_gather | solution.py:13
  105.8 0.1 reshape.25
  105.9 1.7 %while.25 = (s32[]{:T(128)}, f32[8192]{0:T(1024)S(1)}, f32[8192]{0:T(1024)S(1)}, f32[15,8192]{1,0:T(8,128)S(1)}, f32[15,8192]{1,0:T(8,128)S(1)}, /*index=5*/s32[]{:T(128)}) while((s32[]{:T(128)}, f32[8192]{0:T(1024)S(1)}, f32[8192]{0:T(1024)S(1)}, f32[15,8192]{1,0:T(8,128)S(1)}, f32[15,8192]{1,0:T(8,128)S(1)}, /*index=5*/s32[]{:T(128)}) %tuple.51), condition=%wide.region_9.10_spmd, body=%wide.region_8.9_spmd.sunk | while | flops 49154 | bytes 327761 | solution.py:16
  107.6 0.6 broadcast_multiply_fusion
  108.3 4.1 %fusion.13 = f32[256]{0:T(256)S(1)} fusion(bf16[256,8192]{1,0:T(8,128)(2,1)} %param.8, f32[8192]{0:T(1024)S(1)} %get-tuple-element.87, f32[256]{0:T(256)S(1)} %multiply_minimum_fusion.1), kind=kLoop, calls=%fused_computation.21 | loop fusion | flops 12582656 | bytes 4229120 | tf_op jit(solution)/shard_map/reduce_sum | solution.py:48
  112.4 4.9 %psum.15 = f32[256]{0:T(256)S(1)} all-reduce(f32[256]{0:T(256)S(1)} %fusion.13), channel_id=1, replica_groups=mesh['adv'=16,'imp'=2] {'imp'}, use_global_device_ids=true, to_apply=%region_11.12 | all-reduce | flops 256 | bytes 2048 | tf_op jit(solution)/shard_map/psum | solution.py:35
  117.3 0.6 multiply_minimum_fusion
  (68 shorter events, 2.3 us)
Async XLA Ops:
  0.6 3.6 %copy-start.3 = (f32[256]{0:T(256)S(1)}, f32[256]{0:T(256)}, u32[]{:S(2)}) copy-start(f32[256]{0:T(256)} %param.10) | copy-start | bytes 3076
  0.6 3.6 %copy-start = (bf16[256,8192]{1,0:T(8,128)(2,1)S(1)}, bf16[256,8192]{1,0:T(8,128)(2,1)}, u32[]{:S(2)}) copy-start(bf16[256,8192]{1,0:T(8,128)(2,1)} %param.8) | copy-start | bytes 12582916
  6.3 45.5 %copy-start.2 = (f32[8192]{0:T(1024)S(1)}, f32[8192]{0:T(1024)}, u32[]{:S(2)}) copy-start(f32[8192]{0:T(1024)} %param.11) | copy-start | bytes 98308
  49.9 11.0 %copy-start.4 = (f32[256]{0:T(256)S(1)}, f32[256]{0:T(256)}, u32[]{:S(2)}) copy-start(f32[256]{0:T(256)} %param.9) | copy-start | bytes 3076
  60.9 3.6 %copy-start.1 = (bf16[256,8192]{1,0:T(8,128)(2,1)S(1)}, bf16[256,8192]{1,0:T(8,128)(2,1)}, u32[]{:S(2)}) copy-start(bf16[256,8192]{1,0:T(8,128)(2,1)} %param.8) | copy-start | bytes 12582916
where the time goes:
time: 118 us
  blocking collectives  92.5 us (78%)
  other arithmetic  21.8 us (18%)
  local copies, waits for them, and re-layouts  2.12 us (2%)
    all_gather x4, blocking collectives, merged(): pieces = jax.tree.map(lambda part: lax.all_gather(part, axis), value)  82.6 us
    psum x2, blocking collectives, update_pace(): spend = lax.psum(partial_value, 'imp')  9.88 us
    reduce_sum x2, other arithmetic, on_device(): partial_value = jnp.sum(jnp.exp(score - lse[None, :]) * bid, axis=1)  8.2 us
    reduce_max x2, other arithmetic, log_totals(): local_top = jnp.max(score, axis=0)  7.14 us
    reduce_sum x2, other arithmetic, log_totals(): local_sum = jnp.sum(jnp.exp(score - local_top[None, :]), axis=0)  4.02 us

commit v1 on v0

v1 whole, which is shorter than its diff:
```python
import functools
import math

import jax
import jax.numpy as jnp
from jax import lax
from jax.experimental import pallas as pl
from jax.experimental.pallas import tpu as pltpu
from jax.sharding import PartitionSpec as P

ROUNDS = 2
EPS = 0.015
LANES = 128
LOG2E = math.log2(math.e)
LN2 = math.log(2.0)
SCALE = LOG2E / EPS


def kernel(
    n, m, owners,
    values, limits, start, reserve,
    pace_out, price_out,
    held, weighted, column, column16, pace_row, tops, sums, mine, parts, lses, spends,
    load_sem, send_part, recv_part, send_lse, recv_lse, send_spend, recv_spend,
):
    adv, imp = lax.axis_index("adv"), lax.axis_index("imp")
    stride = n // owners
    base = adv // stride
    segs, rows, width = held.shape
    wide = width // LANES
    halves = rows // LANES

    def load(k):
        return pltpu.make_async_copy(
            values.at[:, pl.ds(pl.multiple_of(k * width, width), width)], held.at[k], load_sem.at[k]
        )

    def part_copy(step, k, source, target):
        return pltpu.make_async_remote_copy(
            src_ref=mine.at[step, k], dst_ref=parts.at[step, source],
            send_sem=send_part.at[step, k], recv_sem=recv_part.at[step, source],
            device_id=(target, imp), device_id_type=pl.DeviceIdType.MESH,
        )

    def lse_copy(step, k, target):
        return pltpu.make_async_remote_copy(
            src_ref=lses.at[step, k], dst_ref=lses.at[step, k],
            send_sem=send_lse.at[step, target], recv_sem=recv_lse.at[step, k],
            device_id=(target, imp), device_id_type=pl.DeviceIdType.MESH,
        )

    def spend_copy(step, source, target):
        return pltpu.make_async_remote_copy(
            src_ref=spends.at[step, source], dst_ref=spends.at[step, source],
            send_sem=send_spend.at[step, target], recv_sem=recv_spend.at[step, source],
            device_id=(adv, target), device_id_type=pl.DeviceIdType.MESH,
        )

    @pl.loop(0, owners)
    def _(t):
        load(lax.rem(base + 1 + t, owners)).start()

    barrier = pltpu.get_barrier_semaphore()

    @pl.loop(1, n)
    def _(t):
        pl.semaphore_signal(
            barrier, inc=1, device_id=(lax.rem(adv + t, n), imp), device_id_type=pl.DeviceIdType.MESH
        )

    @pl.loop(1, m)
    def _(t):
        pl.semaphore_signal(
            barrier, inc=1, device_id=(adv, lax.rem(imp + t, m)), device_id_type=pl.DeviceIdType.MESH
        )

    def set_column():
        for h in range(halves):
            spread = jnp.broadcast_to(pace_row[h : h + 1, :], (LANES, LANES)).T * SCALE
            column[h * LANES : (h + 1) * LANES, :] = spread
            column16[h * LANES : (h + 1) * LANES, :] = spread.astype(jnp.bfloat16)

    pace_row[...] = start[...]
    set_column()
    pl.semaphore_wait(barrier, n - 1 + m - 1)

    for step in range(ROUNDS):

        @pl.loop(0, owners)
        def _(t):
            k = lax.rem(base + 1 + t, owners)
            if step == 0:
                load(k).wait()
            for r in range(wide):
                lanes = slice(r * LANES, (r + 1) * LANES)
                value = held[k, :, lanes]
                rough = (value * column16[...]).reshape(rows // 16, 16, LANES)
                top = jnp.max(jnp.max(rough, axis=0).astype(jnp.float32), axis=0, keepdims=True)
                value = value.astype(jnp.float32)
                scaled = jnp.exp2(value * column[...] - top)
                tops[k, r : r + 1, :] = top
                sums[r : r + 1, :] = jnp.sum(scaled, axis=0, keepdims=True)
                weighted[k, :, lanes] = scaled * value
            local = tops[k] + jnp.log(sums[...]) * LOG2E
            owner = k * stride

            @pl.when(owner != adv)
            def _():
                mine[step, k] = local
                part_copy(step, k, adv, owner).start()

            @pl.when(owner == adv)
            def _():
                parts[step, adv] = local

        def own():
            @pl.loop(1, n)
            def _(t):
                part_copy(step, base, lax.rem(adv + n - t, n), adv).wait_recv()

            every = parts[step]
            floor = reserve[base] * SCALE
            upper = jnp.maximum(jnp.max(every, axis=0), floor)
            whole = jnp.sum(jnp.exp2(every - upper[None]), axis=0) + jnp.exp2(floor - upper)
            lses[step, base] = upper + jnp.log(whole) * LOG2E

            @pl.loop(1, n)
            def _(t):
                lse_copy(step, base, lax.rem(adv + t, n)).start()

        if stride == 1:
            own()
        else:
            pl.when(base * stride == adv)(own)

        def gather(t, total):
            k = lax.rem(base + owners - t, owners)

            @pl.when(k * stride != adv)
            def _():
                lse_copy(step, k, adv).wait_recv()

            share = jnp.exp2(tops[k] - lses[step, k])
            for r in range(wide):
                total = total + weighted[k, :, r * LANES : (r + 1) * LANES] * share[r : r + 1, :]
            return total

        total = lax.fori_loop(0, owners, gather, jnp.zeros((rows, LANES), jnp.float32))
        for h in range(halves):
            spends[step, imp, h : h + 1, :] = jnp.sum(
                total[h * LANES : (h + 1) * LANES, :].T, axis=0, keepdims=True
            )

        @pl.loop(1, m)
        def _(t):
            spend_copy(step, imp, lax.rem(imp + t, m)).start()

        if step == ROUNDS - 1:
            price_out[...] = lses[step] * (EPS * LN2)

        @pl.loop(1, m)
        def _(t):
            spend_copy(step, lax.rem(imp + t, m), imp).wait_recv()

        spend = pace_row[...] * jnp.sum(spends[step], axis=0)
        pace_row[...] = jnp.minimum(1.0, pace_row[...] * jnp.sqrt(limits[...] / spend))
        if step < ROUNDS - 1:
            set_column()
    pace_out[...] = pace_row[...]

    for step in range(ROUNDS):

        @pl.loop(0, owners)
        def _(k):
            @pl.when(k * stride != adv)
            def _():
                part_copy(step, k, adv, k * stride).wait_send()

        def sent():
            @pl.loop(1, n)
            def _(t):
                lse_copy(step, base, lax.rem(adv + t, n)).wait_send()

        if stride == 1:
            sent()
        else:
            pl.when(base * stride == adv)(sent)

        @pl.loop(1, m)
        def _(t):
            spend_copy(step, imp, lax.rem(imp + t, m)).wait_send()


def on_device(n, m, values, limits, start_pace, reserve):
    rows, columns = values.shape
    tiles = columns // LANES
    owners = math.gcd(n, tiles)
    wide = tiles // owners
    halves = rows // LANES
    vmem = pl.BlockSpec(memory_space=pltpu.VMEM)
    f32 = jnp.float32
    pace, prices = pl.pallas_call(
        functools.partial(kernel, n, m, owners),
        out_shape=(
            jax.ShapeDtypeStruct((halves, LANES), f32),
            jax.ShapeDtypeStruct((owners, wide, LANES), f32),
        ),
        in_specs=[pl.BlockSpec(memory_space=pl.ANY), vmem, vmem, vmem],
        out_specs=(vmem, vmem),
        scratch_shapes=[
            pltpu.VMEM((owners, rows, wide * LANES), jnp.bfloat16),
            pltpu.VMEM((owners, rows, wide * LANES), f32),
            pltpu.VMEM((rows, LANES), f32),
            pltpu.VMEM((rows, LANES), jnp.bfloat16),
            pltpu.VMEM((halves, LANES), f32),
            pltpu.VMEM((owners, wide, LANES), f32),
            pltpu.VMEM((wide, LANES), f32),
            pltpu.VMEM((ROUNDS, owners, wide, LANES), f32),
            pltpu.VMEM((ROUNDS, n, wide, LANES), f32),
            pltpu.VMEM((ROUNDS, owners, wide, LANES), f32),
            pltpu.VMEM((ROUNDS, m, halves, LANES), f32),
            pltpu.SemaphoreType.DMA((owners,)),
            pltpu.SemaphoreType.DMA((ROUNDS, owners)),
            pltpu.SemaphoreType.DMA((ROUNDS, n)),
            pltpu.SemaphoreType.DMA((ROUNDS, n)),
            pltpu.SemaphoreType.DMA((ROUNDS, owners)),
            pltpu.SemaphoreType.DMA((ROUNDS, m)),
            pltpu.SemaphoreType.DMA((ROUNDS, m)),
        ],
        compiler_params=pltpu.CompilerParams(
            collective_id=0, has_side_effects=True, vmem_limit_bytes=62 * 2**20
        ),
        name="pacing",
    )(
        values,
        limits.reshape(halves, LANES),
        start_pace.reshape(halves, LANES),
        reserve.reshape(owners, wide, LANES),
    )
    return pace.reshape(rows), prices.reshape(columns)


def solution(mesh):
    placed = (P("adv", "imp"), P("adv"), P("adv"), P("imp"))
    body = functools.partial(on_device, mesh.shape["adv"], mesh.shape["imp"])
    return jax.shard_map(
        body, mesh=mesh, in_specs=placed, out_specs=(P("adv"), P("imp")), check_vma=False
    )
```

time: 118 us -> 42.8 us (0.36)
  blocking collectives: 92.5 us -> 0 us
  Pallas kernels: 0 us -> 39.3 us
  other arithmetic: 21.8 us -> 0 us
    all_gather x4 -> x0, blocking collectives: 82.6 us -> none  [merged(): pieces = jax.tree.map(lambda part: lax.all_gather(part, axis), value)]
    pallas_call x0 -> x1, Pallas kernels: none -> 39.3 us  [on_device(): pl.pallas_call(functools.partial(kernel, n, m, owners), out_shape=(jax.Sh...]
    reduce_sum x4 -> x0, other arithmetic: 12.2 us -> none  [the longest x2 8.2 us: on_device(): partial_value = jnp.sum(jnp.exp(score - lse[None, :]) * bid, axis=1)]
    psum x2 -> x0, blocking collectives: 9.88 us -> none  [update_pace(): spend = lax.psum(partial_value, 'imp')]
    reduce_max x2 -> x0, other arithmetic: 7.14 us -> none  [log_totals(): local_top = jnp.max(score, axis=0)]
    unnamed x10 -> x2, local copies, waits for them, and re-layouts: 0.02 us -> 2.6 us
    dynamic_slice x30 -> x0, local copies, waits for them, and re-layouts: 1.59 us -> none  [merged(): lax.scan(lambda subtotal, slab: (join(subtotal, slab), None), head, tail)]
    add x31 -> x0, other arithmetic: 1.18 us -> none  [the longest x30 1.15 us: combine_pair(): first[1] * jnp.exp(first[0] - top) + second[1] * jnp.exp(second[0] - top)]
where the time goes in v1:
time: 42.8 us; the launch traced here: 42.5 us
  Pallas kernels  39.3 us (92%)
  local copies, waits for them, and re-layouts  2.6 us (6%)
  between operations  0.64 us (1%)
    pallas_call x1, Pallas kernels, on_device(): pl.pallas_call(functools.partial(kernel, n, m, owners), out_shape=(jax.Sh...  39.3 us
    unnamed x2, local copies, waits for them, and re-layouts  2.6 us

profile of v1, /device:TPU:0, one launch (start us, length us, event | category | flops | bytes accessed | tf_op | source)
XLA Modules:
  0.0 42.5 jit_solution(2278869521624436887)
XLA Ops:
  0.6 39.3 %pacing.1 = (f32[2,128]{1,0:T(2,128)}, f32[16,4,128]{2,1,0:T(4,128)}) custom-call(bf16[256,8192]{1,0:T(8,128)(2,1)} %values.1, f32[2,128]{1,0:T(2,128)} %bitcast.8, f32[2,128]{1,0:T(2,128)} %bitcast.9, f32[16,4,128]{2,1,0:T(4,128)} %bitcast.5), custom_call_target="tpu_custom_call" | custom-call | tf_op jit(solution)/shard_map/pacing/pallas_call | solution.py:202
  39.9 1.2 %copy.8 = f32[256]{0:T(256)} copy(f32[256]{0:T(256)} %bitcast.7) | data formatting | bytes 2048
  41.1 1.4 %copy.9 = f32[8192]{0:T(1024)} copy(f32[8192]{0:T(1024)} %bitcast.6) | data formatting | bytes 65536

commit v2 on v1

v2 whole, which is shorter than its diff:
```python
import functools
import math

import jax
import jax.numpy as jnp
from jax import lax
from jax.experimental import pallas as pl
from jax.experimental.pallas import tpu as pltpu
from jax.sharding import PartitionSpec as P

ROUNDS = 2
EPS = 0.015
LANES = 128
BATCH = 4
LOG2E = math.log2(math.e)
LN2 = math.log(2.0)
SCALE = LOG2E / EPS


def kernel(
    n, m, owners,
    values, limits, start, reserve,
    pace_out, price_out,
    held, weighted, column, column16, pace_row, tops, shares, mine, parts, lses, spends,
    load_sem, send_part, recv_part, send_lse, recv_lse, send_spend, recv_spend,
):
    adv, imp = lax.axis_index("adv"), lax.axis_index("imp")
    stride = n // owners
    base = adv // stride
    segs, rows, width = held.shape
    wide = width // LANES
    halves = rows // LANES

    def load(k):
        return pltpu.make_async_copy(
            values.at[:, pl.ds(pl.multiple_of(k * width, width), width)], held.at[k], load_sem.at[k]
        )

    def part_copy(step, k, source, target):
        return pltpu.make_async_remote_copy(
            src_ref=mine.at[step, k], dst_ref=parts.at[step, source],
            send_sem=send_part.at[step], recv_sem=recv_part.at[step],
            device_id=(target, imp), device_id_type=pl.DeviceIdType.MESH,
        )

    def lse_copy(step, k, target):
        return pltpu.make_async_remote_copy(
            src_ref=lses.at[step, k], dst_ref=lses.at[step, k],
            send_sem=send_lse.at[step], recv_sem=recv_lse.at[step],
            device_id=(target, imp), device_id_type=pl.DeviceIdType.MESH,
        )

    def spend_copy(step, source, target):
        return pltpu.make_async_remote_copy(
            src_ref=spends.at[step, source], dst_ref=spends.at[step, source],
            send_sem=send_spend.at[step, target], recv_sem=recv_spend.at[step, source],
            device_id=(adv, target), device_id_type=pl.DeviceIdType.MESH,
        )

    is_owner = base * stride == adv
    batch = math.gcd(owners, BATCH)

    def drain(ref, sem, most):
        def wait(count):
            blocks = ref.at[pl.ds(0, count)]
            pltpu.make_async_copy(blocks, blocks, sem).wait()

        if stride == 1:
            wait(most - 1)
        else:
            pl.when(is_owner)(lambda: wait(most - 1))
            pl.when(jnp.logical_not(is_owner))(lambda: wait(most))

    def if_owner(run):
        if stride == 1:
            run()
        else:
            pl.when(is_owner)(run)

    barrier = pltpu.get_barrier_semaphore()

    @pl.loop(1, n, unroll=True)
    def _(t):
        pl.semaphore_signal(
            barrier, inc=1, device_id=(lax.rem(adv + t, n), imp), device_id_type=pl.DeviceIdType.MESH
        )

    @pl.loop(1, m, unroll=True)
    def _(t):
        pl.semaphore_signal(
            barrier, inc=1, device_id=(adv, lax.rem(imp + t, m)), device_id_type=pl.DeviceIdType.MESH
        )

    @pl.loop(0, owners)
    def _(t):
        load(lax.rem(base + 1 + t, owners)).start()

    def set_column():
        for h in range(halves):
            spread = jnp.broadcast_to(pace_row[h : h + 1, :], (LANES, LANES)).T * SCALE
            column[h * LANES : (h + 1) * LANES, :] = spread
            column16[h * LANES : (h + 1) * LANES, :] = spread.astype(jnp.bfloat16)

    pace_row[...] = start[...]
    set_column()

    def segment(step, k):
        for r in range(wide):
            lanes = slice(r * LANES, (r + 1) * LANES)
            value = held[k, :, lanes]
            rough = (value * column16[...]).reshape(rows // 16, 16, LANES)
            top = jnp.max(jnp.max(rough, axis=0).astype(jnp.float32), axis=0, keepdims=True)
            value = value.astype(jnp.float32)
            scaled = jnp.exp2(value * column[...] - top)
            weighted[k, :, lanes] = scaled * value
            tops[k, r : r + 1, :] = top
            mine[step, k, r : r + 1, :] = (
                top + jnp.log(jnp.sum(scaled, axis=0, keepdims=True)) * LOG2E
            )

    def send_segments(step, t0):
        for g in range(batch):
            k = lax.rem(base + 1 + t0 + g, owners)
            if g < batch - 1:
                part_copy(step, k, adv, k * stride).start()
            else:
                pl.when(k * stride != adv)(part_copy(step, k, adv, k * stride).start)

    def compute_segments(step, t0):
        for g in range(batch):
            k = lax.rem(base + 1 + t0 + g, owners)
            if step == 0:
                load(k).wait()
            segment(step, k)

    for step in range(ROUNDS):
        compute_segments(step, 0)
        if step == 0:
            pl.semaphore_wait(barrier, n - 1 + m - 1)
        send_segments(step, 0)

        @pl.loop(batch, owners, step=batch)
        def _(t0):
            compute_segments(step, t0)
            send_segments(step, t0)

        def own():
            parts[step, adv] = mine[step, base]
            blocks = parts.at[step, pl.ds(0, n - 1)]
            pltpu.make_async_copy(blocks, blocks, recv_part.at[step]).wait()
            every = parts[step]
            floor = reserve[base] * SCALE
            upper = jnp.maximum(jnp.max(every, axis=0), floor)
            whole = jnp.sum(jnp.exp2(every - upper[None]), axis=0) + jnp.exp2(floor - upper)
            lses[step, base] = upper + jnp.log(whole) * LOG2E

            @pl.loop(1, n, unroll=True)
            def _(t):
                lse_copy(step, base, lax.rem(adv + t, n)).start()

        if_owner(own)
        drain(mine.at[step], send_part.at[step], owners)
        drain(lses.at[step], recv_lse.at[step], owners)
        shares[...] = jnp.exp2(tops[...] - lses[step])

        def gather(b, total):
            for g in range(batch):
                k = b * batch + g
                for r in range(wide):
                    total = total + weighted[k, :, r * LANES : (r + 1) * LANES] * shares[k, r : r + 1, :]
            return total

        total = lax.fori_loop(0, owners // batch, gather, jnp.zeros((rows, LANES), jnp.float32))
        for h in range(halves):
            spends[step, imp, h : h + 1, :] = jnp.sum(
                total[h * LANES : (h + 1) * LANES, :].T, axis=0, keepdims=True
            )

        @pl.loop(1, m)
        def _(t):
            spend_copy(step, imp, lax.rem(imp + t, m)).start()

        if step == ROUNDS - 1:
            price_out[...] = lses[step] * (EPS * LN2)

        def sent():
            blocks = parts.at[step, pl.ds(0, n - 1)]
            pltpu.make_async_copy(blocks, blocks, send_lse.at[step]).wait()

        if_owner(sent)

        @pl.loop(1, m)
        def _(t):
            spend_copy(step, lax.rem(imp + t, m), imp).wait_recv()

        spend = pace_row[...] * jnp.sum(spends[step], axis=0)
        pace_row[...] = jnp.minimum(1.0, pace_row[...] * jnp.sqrt(limits[...] / spend))
        if step < ROUNDS - 1:
            set_column()

        @pl.loop(1, m)
        def _(t):
            spend_copy(step, imp, lax.rem(imp + t, m)).wait_send()

    pace_out[...] = pace_row[...]


def hand_over(pace, prices, pace_out, price_out, sem):
    copies = [
        pltpu.make_async_copy(prices, price_out, sem.at[0]),
        pltpu.make_async_copy(pace, pace_out, sem.at[1]),
    ]
    for copy in copies:
        copy.start()
    for copy in copies:
        copy.wait()


def on_device(n, m, values, limits, start_pace, reserve):
    rows, columns = values.shape
    tiles = columns // LANES
    owners = math.gcd(n, tiles)
    wide = tiles // owners
    halves = rows // LANES
    vmem = pl.BlockSpec(memory_space=pltpu.VMEM)
    f32 = jnp.float32
    pace, prices = pl.pallas_call(
        functools.partial(kernel, n, m, owners),
        out_shape=(
            jax.ShapeDtypeStruct((halves, LANES), f32),
            jax.ShapeDtypeStruct((owners, wide, LANES), f32),
        ),
        in_specs=[pl.BlockSpec(memory_space=pl.ANY), vmem, vmem, vmem],
        out_specs=(vmem, vmem),
        scratch_shapes=[
            pltpu.VMEM((owners, rows, wide * LANES), jnp.bfloat16),
            pltpu.VMEM((owners, rows, wide * LANES), f32),
            pltpu.VMEM((rows, LANES), f32),
            pltpu.VMEM((rows, LANES), jnp.bfloat16),
            pltpu.VMEM((halves, LANES), f32),
            pltpu.VMEM((owners, wide, LANES), f32),
            pltpu.VMEM((owners, wide, LANES), f32),
            pltpu.VMEM((ROUNDS, owners, wide, LANES), f32),
            pltpu.VMEM((ROUNDS, n, wide, LANES), f32),
            pltpu.VMEM((ROUNDS, owners, wide, LANES), f32),
            pltpu.VMEM((ROUNDS, m, halves, LANES), f32),
            pltpu.SemaphoreType.DMA((owners,)),
            pltpu.SemaphoreType.DMA((ROUNDS,)),
            pltpu.SemaphoreType.DMA((ROUNDS,)),
            pltpu.SemaphoreType.DMA((ROUNDS,)),
            pltpu.SemaphoreType.DMA((ROUNDS,)),
            pltpu.SemaphoreType.DMA((ROUNDS, m)),
            pltpu.SemaphoreType.DMA((ROUNDS, m)),
        ],
        compiler_params=pltpu.CompilerParams(
            collective_id=0, has_side_effects=True, vmem_limit_bytes=62 * 2**20
        ),
        name="pacing",
    )(
        values,
        limits.reshape(halves, LANES),
        start_pace.reshape(halves, LANES),
        reserve.reshape(owners, wide, LANES),
    )
    away = pl.BlockSpec(memory_space=pl.ANY)
    pace, prices = pl.pallas_call(
        hand_over,
        out_shape=(
            jax.ShapeDtypeStruct(pace.shape, f32),
            jax.ShapeDtypeStruct(prices.shape, f32),
        ),
        in_specs=[away, away],
        out_specs=(away, away),
        scratch_shapes=[pltpu.SemaphoreType.DMA((2,))],
        compiler_params=pltpu.CompilerParams(vmem_limit_bytes=62 * 2**20),
        name="hand_over",
    )(pace, prices)
    return pace.reshape(rows), prices.reshape(columns)


def solution(mesh):
    placed = (P("adv", "imp"), P("adv"), P("adv"), P("imp"))
    body = functools.partial(on_device, mesh.shape["adv"], mesh.shape["imp"])
    return jax.shard_map(
        body, mesh=mesh, in_specs=placed, out_specs=(P("adv"), P("imp")), check_vma=False
    )
```

time: 42.8 us -> 39.5 us (0.923)
  local copies, waits for them, and re-layouts: 2.6 us -> 0 us
  Pallas kernels: 39.3 us -> 38.7 us
    pallas_call x1, Pallas kernels: 39.3 us -> 36.6 us  [on_device(): pl.pallas_call(functools.partial(kernel, n, m, owners), out_shape=(jax.Sh...]
    unnamed x2 -> x0, local copies, waits for them, and re-layouts: 2.6 us -> none
    pallas_call x0 -> x1, Pallas kernels: none -> 2.14 us  [on_device(): pl.pallas_call(hand_over, out_shape=(jax.ShapeDtypeStruct(pace.shape, f32...]
where the time goes in v2:
time: 39.5 us; the launch traced here: 39.4 us
  Pallas kernels  38.7 us (98%)
  between operations  0.64 us (2%)
    pallas_call x1, Pallas kernels, on_device(): pl.pallas_call(functools.partial(kernel, n, m, owners), out_shape=(jax.Sh...  36.6 us
    pallas_call x1, Pallas kernels, on_device(): pl.pallas_call(hand_over, out_shape=(jax.ShapeDtypeStruct(pace.shape, f32...  2.14 us

profile of v2, /device:TPU:0, one launch (start us, length us, event | category | flops | bytes accessed | tf_op | source)
XLA Modules:
  0.0 39.4 jit_solution(6836678287647987771)
XLA Ops:
  0.6 36.6 %pacing.1 = (f32[2,128]{1,0:T(2,128)}, f32[16,4,128]{2,1,0:T(4,128)}) custom-call(bf16[256,8192]{1,0:T(8,128)(2,1)} %values.1, f32[2,128]{1,0:T(2,128)} %bitcast.6, f32[2,128]{1,0:T(2,128)} %bitcast.7, f32[16,4,128]{2,1,0:T(4,128)} %bitcast.5), custom_call_target="tpu_custom_call" | custom-call | tf_op jit(solution)/shard_map/pacing/pallas_call | solution.py:227
  37.2 2.1 %hand_over.1 = (f32[2,128]{1,0:T(2,128)}, f32[16,4,128]{2,1,0:T(4,128)}) custom-call(f32[2,128]{1,0:T(2,128)} %get-tuple-element.6.pace, f32[16,4,128]{2,1,0:T(4,128)} %get-tuple-element.7.prices), custom_call_target="tpu_custom_call" | custom-call | tf_op jit(solution)/shard_map/hand_over/pallas_call | solution.py:266

commit v3 on v2

--- a/solution.py
+++ b/solution.py
@@ -21,8 +21,8 @@
     n, m, owners,
     values, limits, start, reserve,
     pace_out, price_out,
-    held, weighted, column, column16, pace_row, tops, shares, mine, parts, lses, spends,
-    load_sem, send_part, recv_part, send_lse, recv_lse, send_spend, recv_spend,
+    held, weighted, column, column16, pace_row, limit_row, floors, tops, shares, mine, parts, lses, spends,
+    small_sem, load_sem, send_part, recv_part, send_lse, recv_lse, send_spend, recv_spend,
 ):
     adv, imp = lax.axis_index("adv"), lax.axis_index("imp")
     stride = n // owners
@@ -46,7 +46,7 @@
     def lse_copy(step, k, target):
         return pltpu.make_async_remote_copy(
             src_ref=lses.at[step, k], dst_ref=lses.at[step, k],
-            send_sem=send_lse.at[step], recv_sem=recv_lse.at[step],
+            send_sem=send_lse.at[step], recv_sem=recv_lse.at[step, k // batch],
             device_id=(target, imp), device_id_type=pl.DeviceIdType.MESH,
         )
 
@@ -60,6 +60,15 @@
     is_owner = base * stride == adv
     batch = math.gcd(owners, BATCH)
 
+    def partner(own, c, size):
+        if size & (size - 1):
+            return lax.rem(own + c, size)
+        bits = [1 << i for i in range(size.bit_length() - 1)]
+        return sum((lax.rem(own // bit + c // bit, 2) * bit for bit in bits), 0)
+
+    def nearest_last(t):
+        return partner(base, owners - 1 - t, owners)
+
     def drain(ref, sem, most):
         def wait(count):
             blocks = ref.at[pl.ds(0, count)]
@@ -91,9 +100,18 @@
             barrier, inc=1, device_id=(adv, lax.rem(imp + t, m)), device_id_type=pl.DeviceIdType.MESH
         )
 
+    small = [
+        pltpu.make_async_copy(source, target, small_sem.at[at])
+        for at, (source, target) in enumerate(((start, pace_row), (limits, limit_row), (reserve, floors)))
+    ]
+    small[0].start()
+
     @pl.loop(0, owners)
     def _(t):
-        load(lax.rem(base + 1 + t, owners)).start()
+        load(nearest_last(t)).start()
+
+    small[1].start()
+    small[2].start()
 
     def set_column():
         for h in range(halves):
@@ -101,7 +119,7 @@
             column[h * LANES : (h + 1) * LANES, :] = spread
             column16[h * LANES : (h + 1) * LANES, :] = spread.astype(jnp.bfloat16)
 
-    pace_row[...] = start[...]
+    small[0].wait()
     set_column()
 
     def segment(step, k):
@@ -120,7 +138,7 @@
 
     def send_segments(step, t0):
         for g in range(batch):
-            k = lax.rem(base + 1 + t0 + g, owners)
+            k = nearest_last(t0 + g)
             if g < batch - 1:
                 part_copy(step, k, adv, k * stride).start()
             else:
@@ -128,7 +146,7 @@
 
     def compute_segments(step, t0):
         for g in range(batch):
-            k = lax.rem(base + 1 + t0 + g, owners)
+            k = nearest_last(t0 + g)
             if step == 0:
                 load(k).wait()
             segment(step, k)
@@ -144,33 +162,47 @@
             compute_segments(step, t0)
             send_segments(step, t0)
 
+        if step == 0:
+            small[1].wait()
+            small[2].wait()
+
         def own():
             parts[step, adv] = mine[step, base]
             blocks = parts.at[step, pl.ds(0, n - 1)]
             pltpu.make_async_copy(blocks, blocks, recv_part.at[step]).wait()
             every = parts[step]
-            floor = reserve[base] * SCALE
+            floor = floors[base] * SCALE
             upper = jnp.maximum(jnp.max(every, axis=0), floor)
             whole = jnp.sum(jnp.exp2(every - upper[None]), axis=0) + jnp.exp2(floor - upper)
             lses[step, base] = upper + jnp.log(whole) * LOG2E
 
             @pl.loop(1, n, unroll=True)
             def _(t):
-                lse_copy(step, base, lax.rem(adv + t, n)).start()
+                lse_copy(step, base, partner(adv, n - t, n)).start()
 
         if_owner(own)
         drain(mine.at[step], send_part.at[step], owners)
-        drain(lses.at[step], recv_lse.at[step], owners)
-        shares[...] = jnp.exp2(tops[...] - lses[step])
-
-        def gather(b, total):
+        groups = owners // batch
+
+        def gather(c, total):
+            group = partner(base // batch, c, groups)
+            first = group * batch
+            if isinstance(c, int):
+                drain(lses.at[step], recv_lse.at[step, group], batch)
+            else:
+                blocks = lses.at[step, pl.ds(0, batch)]
+                pltpu.make_async_copy(blocks, blocks, recv_lse.at[step, group]).wait()
+            members = pl.ds(first, batch)
+            shares[...] = jnp.exp2(tops[members] - lses[step, members])
             for g in range(batch):
-                k = b * batch + g
                 for r in range(wide):
-                    total = total + weighted[k, :, r * LANES : (r + 1) * LANES] * shares[k, r : r + 1, :]
+                    total = total + (
+                        weighted[first + g, :, r * LANES : (r + 1) * LANES] * shares[g, r : r + 1, :]
+                    )
             return total
 
-        total = lax.fori_loop(0, owners // batch, gather, jnp.zeros((rows, LANES), jnp.float32))
+        total = gather(0, jnp.zeros((rows, LANES), jnp.float32))
+        total = lax.fori_loop(1, groups, gather, total)
         for h in range(halves):
             spends[step, imp, h : h + 1, :] = jnp.sum(
                 total[h * LANES : (h + 1) * LANES, :].T, axis=0, keepdims=True
@@ -194,7 +226,7 @@
             spend_copy(step, lax.rem(imp + t, m), imp).wait_recv()
 
         spend = pace_row[...] * jnp.sum(spends[step], axis=0)
-        pace_row[...] = jnp.minimum(1.0, pace_row[...] * jnp.sqrt(limits[...] / spend))
+        pace_row[...] = jnp.minimum(1.0, pace_row[...] * jnp.sqrt(limit_row[...] / spend))
         if step < ROUNDS - 1:
             set_column()
 
@@ -222,6 +254,7 @@
     owners = math.gcd(n, tiles)
     wide = tiles // owners
     halves = rows // LANES
+    batch = math.gcd(owners, BATCH)
     vmem = pl.BlockSpec(memory_space=pltpu.VMEM)
     f32 = jnp.float32
     pace, prices = pl.pallas_call(
@@ -230,7 +263,7 @@
             jax.ShapeDtypeStruct((halves, LANES), f32),
             jax.ShapeDtypeStruct((owners, wide, LANES), f32),
         ),
-        in_specs=[pl.BlockSpec(memory_space=pl.ANY), vmem, vmem, vmem],
+        in_specs=[pl.BlockSpec(memory_space=pltpu.HBM)] * 4,
         out_specs=(vmem, vmem),
         scratch_shapes=[
             pltpu.VMEM((owners, rows, wide * LANES), jnp.bfloat16),
@@ -238,22 +271,25 @@
             pltpu.VMEM((rows, LANES), f32),
             pltpu.VMEM((rows, LANES), jnp.bfloat16),
             pltpu.VMEM((halves, LANES), f32),
+            pltpu.VMEM((halves, LANES), f32),
             pltpu.VMEM((owners, wide, LANES), f32),
             pltpu.VMEM((owners, wide, LANES), f32),
+            pltpu.VMEM((batch, wide, LANES), f32),
             pltpu.VMEM((ROUNDS, owners, wide, LANES), f32),
             pltpu.VMEM((ROUNDS, n, wide, LANES), f32),
             pltpu.VMEM((ROUNDS, owners, wide, LANES), f32),
             pltpu.VMEM((ROUNDS, m, halves, LANES), f32),
+            pltpu.SemaphoreType.DMA((3,)),
             pltpu.SemaphoreType.DMA((owners,)),
             pltpu.SemaphoreType.DMA((ROUNDS,)),
             pltpu.SemaphoreType.DMA((ROUNDS,)),
             pltpu.SemaphoreType.DMA((ROUNDS,)),
-            pltpu.SemaphoreType.DMA((ROUNDS,)),
+            pltpu.SemaphoreType.DMA((ROUNDS, owners // batch)),
             pltpu.SemaphoreType.DMA((ROUNDS, m)),
             pltpu.SemaphoreType.DMA((ROUNDS, m)),
         ],
         compiler_params=pltpu.CompilerParams(
-            collective_id=0, has_side_effects=True, vmem_limit_bytes=62 * 2**20
+            collective_id=0, has_side_effects=True, vmem_limit_bytes=52 * 2**20
         ),
         name="pacing",
     )(
@@ -272,7 +308,6 @@
         in_specs=[away, away],
         out_specs=(away, away),
         scratch_shapes=[pltpu.SemaphoreType.DMA((2,))],
-        compiler_params=pltpu.CompilerParams(vmem_limit_bytes=62 * 2**20),
         name="hand_over",
     )(pace, prices)
     return pace.reshape(rows), prices.reshape(columns)

time: 39.5 us -> 37.6 us (0.952)
  Pallas kernels: 38.7 us -> 33.4 us
  local copies, waits for them, and re-layouts: 0 us -> 3.29 us
    pallas_call x1, Pallas kernels: 36.6 us -> 31.3 us  [on_device(): pl.pallas_call(functools.partial(kernel, n, m, owners), out_shape=(jax.Sh...]
    unnamed x0 -> x10, local copies, waits for them, and re-layouts: none -> 3.29 us
where the time goes in v3:
time: 37.6 us; the launch traced here: 37.4 us
  Pallas kernels  33.4 us (89%)
  local copies, waits for them, and re-layouts  3.29 us (9%)
  between operations  0.66 us (2%)
    pallas_call x1, Pallas kernels, on_device(): pl.pallas_call(functools.partial(kernel, n, m, owners), out_shape=(jax.Sh...  31.3 us
    unnamed x10, local copies, waits for them, and re-layouts  3.29 us
    pallas_call x1, Pallas kernels, on_device(): pl.pallas_call(hand_over, out_shape=(jax.ShapeDtypeStruct(pace.shape, f32...  2.14 us

profile of v3, /device:TPU:0, one launch (start us, length us, event | category | flops | bytes accessed | tf_op | source)
XLA Modules:
  0.0 37.4 jit_solution(2878397806542860385)
XLA Ops:
  0.6 0.0 copy-start
  0.6 0.7 %copy-done = f32[8192]{0:T(1024)S(1)} copy-done((f32[8192]{0:T(1024)S(1)}, f32[8192]{0:T(1024)}, u32[]{:S(2)}) %copy-start) | copy-done | bytes 32792
  1.4 0.0 copy-start.3
  1.4 0.7 %copy-done.3 = f32[256]{0:T(256)S(1)} copy-done((f32[256]{0:T(256)S(1)}, f32[256]{0:T(256)}, u32[]{:S(2)}) %copy-start.3) | copy-done | bytes 1048
  2.1 0.0 copy-start.4
  2.1 0.7 %copy-done.4 = f32[256]{0:T(256)S(1)} copy-done((f32[256]{0:T(256)S(1)}, f32[256]{0:T(256)}, u32[]{:S(2)}) %copy-start.4) | copy-done | bytes 1048
  2.7 31.3 %pacing.1 = (f32[2,128]{1,0:T(2,128)S(1)}, f32[16,4,128]{2,1,0:T(4,128)S(1)}) custom-call(bf16[256,8192]{1,0:T(8,128)(2,1)} %values.1, f32[2,128]{1,0:T(2,128)S(1)} %bitcast.6, f32[2,128]{1,0:T(2,128)S(1)} %bitcast.7, f32[16,4,128]{2,1,0:T(4,128)S(1)} %bitcast.5), custom_call_target="tpu_custom_call" | custom-call | tf_op jit(solution)/shard_map/pacing/pallas_call | solution.py:260
  34.0 0.0 copy-start.1
  34.0 0.6 %copy-done.1 = f32[16,4,128]{2,1,0:T(4,128)} copy-done((f32[16,4,128]{2,1,0:T(4,128)}, f32[16,4,128]{2,1,0:T(4,128)S(1)}, u32[]{:S(2)}) %copy-start.1) | copy-done | bytes 32792
  34.6 0.0 copy-start.2
  34.6 0.6 %copy-done.2 = f32[2,128]{1,0:T(2,128)} copy-done((f32[2,128]{1,0:T(2,128)}, f32[2,128]{1,0:T(2,128)S(1)}, u32[]{:S(2)}) %copy-start.2) | copy-done | bytes 1048
  35.2 2.1 %hand_over.1 = (f32[2,128]{1,0:T(2,128)}, f32[16,4,128]{2,1,0:T(4,128)}) custom-call(f32[2,128]{1,0:T(2,128)} %copy-done.2, f32[16,4,128]{2,1,0:T(4,128)} %copy-done.1), custom_call_target="tpu_custom_call" | custom-call | tf_op jit(solution)/shard_map/hand_over/pallas_call | solution.py:302
Async XLA Ops:
  0.6 0.8 %copy-start = (f32[8192]{0:T(1024)S(1)}, f32[8192]{0:T(1024)}, u32[]{:S(2)}) copy-start(f32[8192]{0:T(1024)} %param.7) | copy-start | bytes 98308
  1.4 0.7 %copy-start.3 = (f32[256]{0:T(256)S(1)}, f32[256]{0:T(256)}, u32[]{:S(2)}) copy-start(f32[256]{0:T(256)} %param.5) | copy-start | bytes 3076
  2.1 0.7 %copy-start.4 = (f32[256]{0:T(256)S(1)}, f32[256]{0:T(256)}, u32[]{:S(2)}) copy-start(f32[256]{0:T(256)} %param.6) | copy-start | bytes 3076
  34.0 0.6 %copy-start.1 = (f32[16,4,128]{2,1,0:T(4,128)}, f32[16,4,128]{2,1,0:T(4,128)S(1)}, u32[]{:S(2)}) copy-start(f32[16,4,128]{2,1,0:T(4,128)S(1)} %get-tuple-element.7.prices) | copy-start | bytes 98308
  34.6 0.6 %copy-start.2 = (f32[2,128]{1,0:T(2,128)}, f32[2,128]{1,0:T(2,128)S(1)}, u32[]{:S(2)}) copy-start(f32[2,128]{1,0:T(2,128)S(1)} %get-tuple-element.6.pace) | copy-start | bytes 3076

commit v4 on v3

--- a/solution.py
+++ b/solution.py
@@ -21,8 +21,8 @@
     n, m, owners,
     values, limits, start, reserve,
     pace_out, price_out,
-    held, weighted, column, column16, pace_row, limit_row, floors, tops, shares, mine, parts, lses, spends,
-    small_sem, load_sem, send_part, recv_part, send_lse, recv_lse, send_spend, recv_spend,
+    held, weighted, column, column16, pace_row, limit_row, floors, price_row, tops, shares, mine, parts, lses, spends,
+    small_sem, out_sem, load_sem, send_part, recv_part, send_lse, recv_lse, send_spend, recv_spend,
 ):
     adv, imp = lax.axis_index("adv"), lax.axis_index("imp")
     stride = n // owners
@@ -86,27 +86,31 @@
         else:
             pl.when(is_owner)(run)
 
-    barrier = pltpu.get_barrier_semaphore()
-
-    @pl.loop(1, n, unroll=True)
-    def _(t):
-        pl.semaphore_signal(
-            barrier, inc=1, device_id=(lax.rem(adv + t, n), imp), device_id_type=pl.DeviceIdType.MESH
-        )
-
-    @pl.loop(1, m, unroll=True)
-    def _(t):
-        pl.semaphore_signal(
-            barrier, inc=1, device_id=(adv, lax.rem(imp + t, m)), device_id_type=pl.DeviceIdType.MESH
-        )
-
     small = [
         pltpu.make_async_copy(source, target, small_sem.at[at])
         for at, (source, target) in enumerate(((start, pace_row), (limits, limit_row), (reserve, floors)))
     ]
     small[0].start()
 
-    @pl.loop(0, owners)
+    @pl.loop(0, batch, unroll=True)
+    def _(t):
+        load(nearest_last(t)).start()
+
+    barrier = pltpu.get_barrier_semaphore()
+
+    @pl.loop(1, n, unroll=True)
+    def _(t):
+        pl.semaphore_signal(
+            barrier, inc=1, device_id=(lax.rem(adv + t, n), imp), device_id_type=pl.DeviceIdType.MESH
+        )
+
+    @pl.loop(1, m, unroll=True)
+    def _(t):
+        pl.semaphore_signal(
+            barrier, inc=1, device_id=(adv, lax.rem(imp + t, m)), device_id_type=pl.DeviceIdType.MESH
+        )
+
+    @pl.loop(batch, owners, unroll=True)
     def _(t):
         load(nearest_last(t)).start()
 
@@ -213,7 +217,9 @@
             spend_copy(step, imp, lax.rem(imp + t, m)).start()
 
         if step == ROUNDS - 1:
-            price_out[...] = lses[step] * (EPS * LN2)
+            price_row[...] = lses[step] * (EPS * LN2)
+            price_copy = pltpu.make_async_copy(price_row, price_out, out_sem.at[0])
+            price_copy.start()
 
         def sent():
             blocks = parts.at[step, pl.ds(0, n - 1)]
@@ -230,22 +236,21 @@
         if step < ROUNDS - 1:
             set_column()
 
+    pace_copy = pltpu.make_async_copy(pace_row, pace_out, out_sem.at[1])
+    pace_copy.start()
+    for step in range(ROUNDS):
+
         @pl.loop(1, m)
         def _(t):
             spend_copy(step, imp, lax.rem(imp + t, m)).wait_send()
 
-    pace_out[...] = pace_row[...]
-
-
-def hand_over(pace, prices, pace_out, price_out, sem):
-    copies = [
-        pltpu.make_async_copy(prices, price_out, sem.at[0]),
-        pltpu.make_async_copy(pace, pace_out, sem.at[1]),
-    ]
-    for copy in copies:
-        copy.start()
-    for copy in copies:
-        copy.wait()
+    price_copy.wait()
+    pace_copy.wait()
+
+
+def hand_over(pace, prices, pace_out, price_out):
+    pace_out[...] = pace[...]
+    price_out[...] = prices[...]
 
 
 def on_device(n, m, values, limits, start_pace, reserve):
@@ -256,6 +261,7 @@
     halves = rows // LANES
     batch = math.gcd(owners, BATCH)
     vmem = pl.BlockSpec(memory_space=pltpu.VMEM)
+    away = pl.BlockSpec(memory_space=pltpu.HBM)
     f32 = jnp.float32
     pace, prices = pl.pallas_call(
         functools.partial(kernel, n, m, owners),
@@ -263,8 +269,8 @@
             jax.ShapeDtypeStruct((halves, LANES), f32),
             jax.ShapeDtypeStruct((owners, wide, LANES), f32),
         ),
-        in_specs=[pl.BlockSpec(memory_space=pltpu.HBM)] * 4,
-        out_specs=(vmem, vmem),
+        in_specs=[away] * 4,
+        out_specs=(away, away),
         scratch_shapes=[
             pltpu.VMEM((owners, rows, wide * LANES), jnp.bfloat16),
             pltpu.VMEM((owners, rows, wide * LANES), f32),
@@ -274,12 +280,14 @@
             pltpu.VMEM((halves, LANES), f32),
             pltpu.VMEM((owners, wide, LANES), f32),
             pltpu.VMEM((owners, wide, LANES), f32),
+            pltpu.VMEM((owners, wide, LANES), f32),
             pltpu.VMEM((batch, wide, LANES), f32),
             pltpu.VMEM((ROUNDS, owners, wide, LANES), f32),
             pltpu.VMEM((ROUNDS, n, wide, LANES), f32),
             pltpu.VMEM((ROUNDS, owners, wide, LANES), f32),
             pltpu.VMEM((ROUNDS, m, halves, LANES), f32),
             pltpu.SemaphoreType.DMA((3,)),
+            pltpu.SemaphoreType.DMA((2,)),
             pltpu.SemaphoreType.DMA((owners,)),
             pltpu.SemaphoreType.DMA((ROUNDS,)),
             pltpu.SemaphoreType.DMA((ROUNDS,)),
@@ -289,7 +297,7 @@
             pltpu.SemaphoreType.DMA((ROUNDS, m)),
         ],
         compiler_params=pltpu.CompilerParams(
-            collective_id=0, has_side_effects=True, vmem_limit_bytes=52 * 2**20
+            collective_id=0, has_side_effects=True, vmem_limit_bytes=62 * 2**20
         ),
         name="pacing",
     )(
@@ -298,16 +306,15 @@
         start_pace.reshape(halves, LANES),
         reserve.reshape(owners, wide, LANES),
     )
-    away = pl.BlockSpec(memory_space=pl.ANY)
     pace, prices = pl.pallas_call(
         hand_over,
         out_shape=(
             jax.ShapeDtypeStruct(pace.shape, f32),
             jax.ShapeDtypeStruct(prices.shape, f32),
         ),
-        in_specs=[away, away],
-        out_specs=(away, away),
-        scratch_shapes=[pltpu.SemaphoreType.DMA((2,))],
+        in_specs=[vmem, vmem],
+        out_specs=(vmem, vmem),
+        compiler_params=pltpu.CompilerParams(vmem_limit_bytes=62 * 2**20),
         name="hand_over",
     )(pace, prices)
     return pace.reshape(rows), prices.reshape(columns)

time: 37.6 us -> 34.1 us (0.907)
  local copies, waits for them, and re-layouts: 3.29 us -> 0 us
    unnamed x10 -> x0, local copies, waits for them, and re-layouts: 3.29 us -> none
    pallas_call x1, Pallas kernels: 2.14 us -> 1.38 us  [on_device(): pl.pallas_call(hand_over, out_shape=(jax.ShapeDtypeStruct(pace.shape, f32...]
    pallas_call x1, Pallas kernels: 31.3 us -> 31.9 us  [on_device(): pl.pallas_call(functools.partial(kernel, n, m, owners), out_shape=(jax.Sh...]
where the time goes in v4:
time: 34.1 us; the launch traced here: 33.9 us
  Pallas kernels  33.3 us (98%)
  between operations  0.64 us (2%)
    pallas_call x1, Pallas kernels, on_device(): pl.pallas_call(functools.partial(kernel, n, m, owners), out_shape=(jax.Sh...  31.9 us
    pallas_call x1, Pallas kernels, on_device(): pl.pallas_call(hand_over, out_shape=(jax.ShapeDtypeStruct(pace.shape, f32...  1.38 us

profile of v4, /device:TPU:0, one launch (start us, length us, event | category | flops | bytes accessed | tf_op | source)
XLA Modules:
  0.0 33.9 jit_solution(7532822030068358731)
XLA Ops:
  0.6 31.9 %pacing.1 = (f32[2,128]{1,0:T(2,128)}, f32[16,4,128]{2,1,0:T(4,128)}) custom-call(bf16[256,8192]{1,0:T(8,128)(2,1)} %values.1, f32[2,128]{1,0:T(2,128)} %bitcast.6, f32[2,128]{1,0:T(2,128)} %bitcast.7, f32[16,4,128]{2,1,0:T(4,128)} %bitcast.5), custom_call_target="tpu_custom_call" | custom-call | tf_op jit(solution)/shard_map/pacing/pallas_call | solution.py:266
  32.6 1.4 %hand_over.1 = (f32[2,128]{1,0:T(2,128)}, f32[16,4,128]{2,1,0:T(4,128)}) custom-call(f32[2,128]{1,0:T(2,128)} %get-tuple-element.6.pace, f32[16,4,128]{2,1,0:T(4,128)} %get-tuple-element.7.prices), custom_call_target="tpu_custom_call" | custom-call | tf_op jit(solution)/shard_map/hand_over/pallas_call | solution.py:309

commit v5 on v4

--- a/solution.py
+++ b/solution.py
@@ -30,6 +30,7 @@
     segs, rows, width = held.shape
     wide = width // LANES
     halves = rows // LANES
+    batch = math.gcd(owners, BATCH)
 
     def load(k):
         return pltpu.make_async_copy(
@@ -58,16 +59,25 @@
         )
 
     is_owner = base * stride == adv
-    batch = math.gcd(owners, BATCH)
-
-    def partner(own, c, size):
+
+    def bit_steps(own, size):
+        return [(1 - 2 * lax.rem(lax.div(own, 1 << i), 2)) << i for i in range(size.bit_length() - 1)]
+
+    def partner(own, steps, c, size):
         if size & (size - 1):
             return lax.rem(own + c, size)
-        bits = [1 << i for i in range(size.bit_length() - 1)]
-        return sum((lax.rem(own // bit + c // bit, 2) * bit for bit in bits), 0)
-
-    def nearest_last(t):
-        return partner(base, owners - 1 - t, owners)
+        if isinstance(c, int):
+            return own + sum((step for i, step in enumerate(steps) if c >> i & 1), 0)
+        return own + sum((step * lax.rem(lax.div(c, 1 << i), 2) for i, step in enumerate(steps)), 0)
+
+    groups = owners // batch
+    home, seat = lax.div(base, batch), lax.rem(base, batch)
+    home_steps, seat_steps = bit_steps(home, groups), bit_steps(seat, batch)
+    adv_steps = bit_steps(adv, n)
+
+    def members(b):
+        first = partner(home, home_steps, groups - 1 - b, groups) * batch
+        return [first + partner(seat, seat_steps, batch - 1 - g, batch) for g in range(batch)]
 
     def drain(ref, sem, most):
         def wait(count):
@@ -92,9 +102,8 @@
     ]
     small[0].start()
 
-    @pl.loop(0, batch, unroll=True)
-    def _(t):
-        load(nearest_last(t)).start()
+    for k in members(0):
+        load(k).start()
 
     barrier = pltpu.get_barrier_semaphore()
 
@@ -110,9 +119,10 @@
             barrier, inc=1, device_id=(adv, lax.rem(imp + t, m)), device_id_type=pl.DeviceIdType.MESH
         )
 
-    @pl.loop(batch, owners, unroll=True)
-    def _(t):
-        load(nearest_last(t)).start()
+    @pl.loop(1, groups)
+    def _(b):
+        for k in members(b):
+            load(k).start()
 
     small[1].start()
     small[2].start()
@@ -125,6 +135,8 @@
 
     small[0].wait()
     set_column()
+
+    price_copy = pltpu.make_async_copy(price_row, price_out, out_sem.at[0])
 
     def segment(step, k):
         for r in range(wide):
@@ -140,33 +152,30 @@
                 top + jnp.log(jnp.sum(scaled, axis=0, keepdims=True)) * LOG2E
             )
 
-    def send_segments(step, t0):
-        for g in range(batch):
-            k = nearest_last(t0 + g)
-            if g < batch - 1:
+    @pl.loop(0, ROUNDS)
+    def _(step):
+        @pl.loop(0, groups)
+        def _(b):
+            ks = members(b)
+
+            @pl.when(step == 0)
+            def _():
+                for k in ks:
+                    load(k).wait()
+
+            for k in ks:
+                segment(step, k)
+
+            @pl.when(jnp.logical_and(step == 0, b == 0))
+            def _():
+                pl.semaphore_wait(barrier, n - 1 + m - 1)
+
+            for k in ks[:-1]:
                 part_copy(step, k, adv, k * stride).start()
-            else:
-                pl.when(k * stride != adv)(part_copy(step, k, adv, k * stride).start)
-
-    def compute_segments(step, t0):
-        for g in range(batch):
-            k = nearest_last(t0 + g)
-            if step == 0:
-                load(k).wait()
-            segment(step, k)
-
-    for step in range(ROUNDS):
-        compute_segments(step, 0)
-        if step == 0:
-            pl.semaphore_wait(barrier, n - 1 + m - 1)
-        send_segments(step, 0)
-
-        @pl.loop(batch, owners, step=batch)
-        def _(t0):
-            compute_segments(step, t0)
-            send_segments(step, t0)
-
-        if step == 0:
+            pl.when(ks[-1] * stride != adv)(part_copy(step, ks[-1], adv, ks[-1] * stride).start)
+
+        @pl.when(step == 0)
+        def _():
             small[1].wait()
             small[2].wait()
 
@@ -180,24 +189,26 @@
             whole = jnp.sum(jnp.exp2(every - upper[None]), axis=0) + jnp.exp2(floor - upper)
             lses[step, base] = upper + jnp.log(whole) * LOG2E
 
-            @pl.loop(1, n, unroll=True)
-            def _(t):
-                lse_copy(step, base, partner(adv, n - t, n)).start()
+            for c in range(n - 1, 0, -1):
+                lse_copy(step, base, partner(adv, adv_steps, c, n)).start()
 
         if_owner(own)
         drain(mine.at[step], send_part.at[step], owners)
-        groups = owners // batch
-
         def gather(c, total):
-            group = partner(base // batch, c, groups)
+            group = partner(home, home_steps, c, groups)
             first = group * batch
-            if isinstance(c, int):
+
+            @pl.when(c == 0)
+            def _():
                 drain(lses.at[step], recv_lse.at[step, group], batch)
-            else:
+
+            @pl.when(c > 0)
+            def _():
                 blocks = lses.at[step, pl.ds(0, batch)]
                 pltpu.make_async_copy(blocks, blocks, recv_lse.at[step, group]).wait()
-            members = pl.ds(first, batch)
-            shares[...] = jnp.exp2(tops[members] - lses[step, members])
+
+            here = pl.ds(first, batch)
+            shares[...] = jnp.exp2(tops[here] - lses[step, here])
             for g in range(batch):
                 for r in range(wide):
                     total = total + (
@@ -205,8 +216,7 @@
                     )
             return total
 
-        total = gather(0, jnp.zeros((rows, LANES), jnp.float32))
-        total = lax.fori_loop(1, groups, gather, total)
+        total = lax.fori_loop(0, groups, gather, jnp.zeros((rows, LANES), jnp.float32))
         for h in range(halves):
             spends[step, imp, h : h + 1, :] = jnp.sum(
                 total[h * LANES : (h + 1) * LANES, :].T, axis=0, keepdims=True
@@ -216,9 +226,9 @@
         def _(t):
             spend_copy(step, imp, lax.rem(imp + t, m)).start()
 
-        if step == ROUNDS - 1:
+        @pl.when(step == ROUNDS - 1)
+        def _():
             price_row[...] = lses[step] * (EPS * LN2)
-            price_copy = pltpu.make_async_copy(price_row, price_out, out_sem.at[0])
             price_copy.start()
 
         def sent():
@@ -233,8 +243,7 @@
 
         spend = pace_row[...] * jnp.sum(spends[step], axis=0)
         pace_row[...] = jnp.minimum(1.0, pace_row[...] * jnp.sqrt(limit_row[...] / spend))
-        if step < ROUNDS - 1:
-            set_column()
+        pl.when(step < ROUNDS - 1)(set_column)
 
     pace_copy = pltpu.make_async_copy(pace_row, pace_out, out_sem.at[1])
     pace_copy.start()

time: 34.1 us -> 33.8 us (level)
  Pallas kernels: 33.3 us -> 32.9 us
    pallas_call x1, Pallas kernels: 31.9 us -> 31.5 us  [on_device(): pl.pallas_call(functools.partial(kernel, n, m, owners), out_shape=(jax.Sh...]
where the time goes in v5:
time: 33.8 us; the launch traced here: 33.6 us
  Pallas kernels  32.9 us (97%)
  between operations  0.64 us (2%)
    pallas_call x1, Pallas kernels, on_device(): pl.pallas_call(functools.partial(kernel, n, m, owners), out_shape=(jax.Sh...  31.5 us
    pallas_call x1, Pallas kernels, on_device(): pl.pallas_call(hand_over, out_shape=(jax.ShapeDtypeStruct(pace.shape, f32...  1.38 us

profile of v5, /device:TPU:0, one launch (start us, length us, event | category | flops | bytes accessed | tf_op | source)
XLA Modules:
  0.0 33.6 jit_solution(4137720482101507763)
XLA Ops:
  0.6 31.5 %pacing.1 = (f32[2,128]{1,0:T(2,128)}, f32[16,4,128]{2,1,0:T(4,128)}) custom-call(bf16[256,8192]{1,0:T(8,128)(2,1)} %values.1, f32[2,128]{1,0:T(2,128)} %bitcast.6, f32[2,128]{1,0:T(2,128)} %bitcast.7, f32[16,4,128]{2,1,0:T(4,128)} %bitcast.5), custom_call_target="tpu_custom_call" | custom-call | tf_op jit(solution)/shard_map/pacing/pallas_call | solution.py:275
  32.2 1.4 %hand_over.1 = (f32[2,128]{1,0:T(2,128)}, f32[16,4,128]{2,1,0:T(4,128)}) custom-call(f32[2,128]{1,0:T(2,128)} %get-tuple-element.6.pace, f32[16,4,128]{2,1,0:T(4,128)} %get-tuple-element.7.prices), custom_call_target="tpu_custom_call" | custom-call | tf_op jit(solution)/shard_map/hand_over/pallas_call | solution.py:318

commit v6 on v5

--- a/solution.py
+++ b/solution.py
@@ -12,6 +12,7 @@
 EPS = 0.015
 LANES = 128
 BATCH = 4
+TALL = 64
 LOG2E = math.log2(math.e)
 LN2 = math.log(2.0)
 SCALE = LOG2E / EPS
@@ -138,18 +139,25 @@
 
     price_copy = pltpu.make_async_copy(price_row, price_out, out_sem.at[0])
 
+    tall = math.gcd(rows, TALL)
+    blocks = [slice(at, at + tall) for at in range(0, rows, tall)]
+
     def segment(step, k):
         for r in range(wide):
             lanes = slice(r * LANES, (r + 1) * LANES)
-            value = held[k, :, lanes]
-            rough = (value * column16[...]).reshape(rows // 16, 16, LANES)
-            top = jnp.max(jnp.max(rough, axis=0).astype(jnp.float32), axis=0, keepdims=True)
-            value = value.astype(jnp.float32)
-            scaled = jnp.exp2(value * column[...] - top)
-            weighted[k, :, lanes] = scaled * value
+            rough = held[k, blocks[0], lanes] * column16[blocks[0], :]
+            for block in blocks[1:]:
+                rough = jnp.maximum(rough, held[k, block, lanes] * column16[block, :])
+            top = jnp.max(rough.astype(jnp.float32), axis=0, keepdims=True)
+            tally = jnp.zeros((8, LANES), jnp.float32)
+            for block in blocks:
+                value = held[k, block, lanes].astype(jnp.float32)
+                scaled = jnp.exp2(value * column[block, :] - top)
+                weighted[k, block, lanes] = scaled * value
+                tally = tally + jnp.sum(scaled.reshape(-1, 8, LANES), axis=0)
             tops[k, r : r + 1, :] = top
             mine[step, k, r : r + 1, :] = (
-                top + jnp.log(jnp.sum(scaled, axis=0, keepdims=True)) * LOG2E
+                top + jnp.log(jnp.sum(tally, axis=0, keepdims=True)) * LOG2E
             )
 
     @pl.loop(0, ROUNDS)
@@ -204,19 +212,23 @@
 
             @pl.when(c > 0)
             def _():
-                blocks = lses.at[step, pl.ds(0, batch)]
-                pltpu.make_async_copy(blocks, blocks, recv_lse.at[step, group]).wait()
+                every = lses.at[step, pl.ds(0, batch)]
+                pltpu.make_async_copy(every, every, recv_lse.at[step, group]).wait()
 
             here = pl.ds(first, batch)
             shares[...] = jnp.exp2(tops[here] - lses[step, here])
-            for g in range(batch):
-                for r in range(wide):
-                    total = total + (
-                        weighted[first + g, :, r * LANES : (r + 1) * LANES] * shares[g, r : r + 1, :]
-                    )
-            return total
-
-        total = lax.fori_loop(0, groups, gather, jnp.zeros((rows, LANES), jnp.float32))
+            sums = []
+            for block, part in zip(blocks, total):
+                for g in range(batch):
+                    for r in range(wide):
+                        lanes = slice(r * LANES, (r + 1) * LANES)
+                        part = part + weighted[first + g, block, lanes] * shares[g, r : r + 1, :]
+                sums.append(part)
+            return tuple(sums)
+
+        nothing = jnp.zeros((tall, LANES), jnp.float32)
+        total = lax.fori_loop(0, groups, gather, (nothing,) * len(blocks))
+        total = jnp.concatenate(total, axis=0)
         for h in range(halves):
             spends[step, imp, h : h + 1, :] = jnp.sum(
                 total[h * LANES : (h + 1) * LANES, :].T, axis=0, keepdims=True

time: 33.8 us -> 33 us (0.976)
  Pallas kernels: 32.9 us -> 32.2 us
    pallas_call x1, Pallas kernels: 31.5 us -> 30.8 us  [on_device(): pl.pallas_call(functools.partial(kernel, n, m, owners), out_shape=(jax.Sh...]
where the time goes in v6:
time: 33 us; the launch traced here: 32.8 us
  Pallas kernels  32.2 us (98%)
  between operations  0.64 us (2%)
    pallas_call x1, Pallas kernels, on_device(): pl.pallas_call(functools.partial(kernel, n, m, owners), out_shape=(jax.Sh...  30.8 us
    pallas_call x1, Pallas kernels, on_device(): pl.pallas_call(hand_over, out_shape=(jax.ShapeDtypeStruct(pace.shape, f32...  1.38 us

profile of v6, /device:TPU:0, one launch (start us, length us, event | category | flops | bytes accessed | tf_op | source)
XLA Modules:
  0.0 32.8 jit_solution(15026686992991339596)
XLA Ops:
  0.6 30.8 %pacing.1 = (f32[2,128]{1,0:T(2,128)}, f32[16,4,128]{2,1,0:T(4,128)}) custom-call(bf16[256,8192]{1,0:T(8,128)(2,1)} %values.1, f32[2,128]{1,0:T(2,128)} %bitcast.6, f32[2,128]{1,0:T(2,128)} %bitcast.7, f32[16,4,128]{2,1,0:T(4,128)} %bitcast.5), custom_call_target="tpu_custom_call" | custom-call | tf_op jit(solution)/shard_map/pacing/pallas_call | solution.py:287
  31.4 1.4 %hand_over.1 = (f32[2,128]{1,0:T(2,128)}, f32[16,4,128]{2,1,0:T(4,128)}) custom-call(f32[2,128]{1,0:T(2,128)} %get-tuple-element.6.pace, f32[16,4,128]{2,1,0:T(4,128)} %get-tuple-element.7.prices), custom_call_target="tpu_custom_call" | custom-call | tf_op jit(solution)/shard_map/hand_over/pallas_call | solution.py:330

commit v7 on v6

--- a/solution.py
+++ b/solution.py
@@ -11,7 +11,7 @@
 ROUNDS = 2
 EPS = 0.015
 LANES = 128
-BATCH = 4
+BATCH = 2
 TALL = 64
 LOG2E = math.log2(math.e)
 LN2 = math.log(2.0)

time: 33 us -> 32.8 us (level)
  no operation moved by 1% of the time
where the time goes in v7:
time: 32.8 us; the launch traced here: 32.6 us
  Pallas kernels  32 us (98%)
  between operations  0.64 us (2%)
    pallas_call x1, Pallas kernels, on_device(): pl.pallas_call(functools.partial(kernel, n, m, owners), out_shape=(jax.Sh...  30.6 us
    pallas_call x1, Pallas kernels, on_device(): pl.pallas_call(hand_over, out_shape=(jax.ShapeDtypeStruct(pace.shape, f32...  1.38 us

profile of v7, /device:TPU:0, one launch (start us, length us, event | category | flops | bytes accessed | tf_op | source)
XLA Modules:
  0.0 32.6 jit_solution(1783334484524280381)
XLA Ops:
  0.6 30.6 %pacing.1 = (f32[2,128]{1,0:T(2,128)}, f32[16,4,128]{2,1,0:T(4,128)}) custom-call(bf16[256,8192]{1,0:T(8,128)(2,1)} %values.1, f32[2,128]{1,0:T(2,128)} %bitcast.6, f32[2,128]{1,0:T(2,128)} %bitcast.7, f32[16,4,128]{2,1,0:T(4,128)} %bitcast.5), custom_call_target="tpu_custom_call" | custom-call | tf_op jit(solution)/shard_map/pacing/pallas_call | solution.py:287
  31.2 1.4 %hand_over.1 = (f32[2,128]{1,0:T(2,128)}, f32[16,4,128]{2,1,0:T(4,128)}) custom-call(f32[2,128]{1,0:T(2,128)} %get-tuple-element.6.pace, f32[16,4,128]{2,1,0:T(4,128)} %get-tuple-element.7.prices), custom_call_target="tpu_custom_call" | custom-call | tf_op jit(solution)/shard_map/hand_over/pallas_call | solution.py:330

commit v8 on v7

--- a/solution.py
+++ b/solution.py
@@ -72,6 +72,7 @@
         return own + sum((step * lax.rem(lax.div(c, 1 << i), 2) for i, step in enumerate(steps)), 0)
 
     groups = owners // batch
+    late = max(groups // 2 - 1, 0)
     home, seat = lax.div(base, batch), lax.rem(base, batch)
     home_steps, seat_steps = bit_steps(home, groups), bit_steps(seat, batch)
     adv_steps = bit_steps(adv, n)
@@ -174,13 +175,20 @@
             for k in ks:
                 segment(step, k)
 
-            @pl.when(jnp.logical_and(step == 0, b == 0))
+            @pl.when(jnp.logical_and(step == 0, b == late))
             def _():
                 pl.semaphore_wait(barrier, n - 1 + m - 1)
 
-            for k in ks[:-1]:
-                part_copy(step, k, adv, k * stride).start()
-            pl.when(ks[-1] * stride != adv)(part_copy(step, ks[-1], adv, ks[-1] * stride).start)
+                @pl.loop(0, late)
+                def _(e):
+                    for k in members(e):
+                        part_copy(step, k, adv, k * stride).start()
+
+            @pl.when(jnp.logical_or(step > 0, b >= late))
+            def _():
+                for k in ks[:-1]:
+                    part_copy(step, k, adv, k * stride).start()
+                pl.when(ks[-1] * stride != adv)(part_copy(step, ks[-1], adv, ks[-1] * stride).start)
 
         @pl.when(step == 0)
         def _():

time: 32.8 us -> 31.8 us (0.970)
  Pallas kernels: 32 us -> 31 us
    pallas_call x1, Pallas kernels: 30.6 us -> 29.6 us  [on_device(): pl.pallas_call(functools.partial(kernel, n, m, owners), out_shape=(jax.Sh...]
where the time goes in v8:
time: 31.8 us; the launch traced here: 31.6 us
  Pallas kernels  31 us (97%)
  between operations  0.64 us (2%)
    pallas_call x1, Pallas kernels, on_device(): pl.pallas_call(functools.partial(kernel, n, m, owners), out_shape=(jax.Sh...  29.6 us
    pallas_call x1, Pallas kernels, on_device(): pl.pallas_call(hand_over, out_shape=(jax.ShapeDtypeStruct(pace.shape, f32...  1.38 us

profile of v8, /device:TPU:0, one launch (start us, length us, event | category | flops | bytes accessed | tf_op | source)
XLA Modules:
  0.0 31.6 jit_solution(8763150625023877666)
XLA Ops:
  0.6 29.6 %pacing.1 = (f32[2,128]{1,0:T(2,128)}, f32[16,4,128]{2,1,0:T(4,128)}) custom-call(bf16[256,8192]{1,0:T(8,128)(2,1)} %values.1, f32[2,128]{1,0:T(2,128)} %bitcast.6, f32[2,128]{1,0:T(2,128)} %bitcast.7, f32[16,4,128]{2,1,0:T(4,128)} %bitcast.5), custom_call_target="tpu_custom_call" | custom-call | tf_op jit(solution)/shard_map/pacing/pallas_call | solution.py:295
  30.2 1.4 %hand_over.1 = (f32[2,128]{1,0:T(2,128)}, f32[16,4,128]{2,1,0:T(4,128)}) custom-call(f32[2,128]{1,0:T(2,128)} %get-tuple-element.6.pace, f32[16,4,128]{2,1,0:T(4,128)} %get-tuple-element.7.prices), custom_call_target="tpu_custom_call" | custom-call | tf_op jit(solution)/shard_map/hand_over/pallas_call | solution.py:338
